TPU v7x, 512 devices: a whole 4x4x16 slice. The times are simulated.
512 devices in a mesh: seq: 64 (over z, y_lo, core), grp: 8 (over x, y_hi).
Axes of the slice: x: 4, y: 4 (y_hi: 2, y_lo: 2; y = y_hi * 2 + y_lo), z: 16, core: 2. Of those that a mesh axis runs over, the one named last changes fastest.
Arguments:
- conditioning: bfloat16 [32, 3072], replicated, may hold values from -6 to 6
- mod_weight: bfloat16 [3072, 6144], P(None, ('seq', 'grp')), may hold values from -0.109375 to 0.109375
- mod_bias: float32 [6144], P(('seq', 'grp')), may hold values from -12 to 12
- hidden: bfloat16 [32, 4096, 3072], P('grp', 'seq'), may hold values from -6 to 6
- proj_weight: bfloat16 [3072, 64], replicated, may hold values from -0.109375 to 0.109375
- proj_bias: float32 [64], replicated, may hold values from -3 to 3
- noisy_latent: bfloat16 [32, 128, 128, 16], P('grp', 'seq'), may hold values from -64 to 64
- in_weight: bfloat16 [144, 512], replicated, may hold values from -0.5 to 0.5
- in_bias: float32 [512], replicated, may hold values from -3 to 3
- norm_gain: float32 [512], replicated, may hold values from 0.1 to 1.9
- norm_shift: float32 [512], replicated, may hold values from -3 to 3
- conv_weight: bfloat16 [4608, 512], P('seq'), may hold values from -0.09375 to 0.09375
- conv_bias: float32 [512], replicated, may hold values from -3 to 3
Outputs:
- decoded: bfloat16 [32, 128, 128, 512], P('grp', 'seq')
All inputs are finite; a program needn't handle non-finite values.
Results may differ from a plain program's by a relative error of at most 0.01.
Values may be sent and summed in bfloat16 or wider, within the bound.
A program may use at most 64 MiB of HBM per device.

v0:
```python
import jax
import jax.numpy as jnp
from jax import lax
from jax.sharding import PartitionSpec as P

GROUPS = 32


def padded_2(cells, sides, width):
    for axis, dim in sides:
        count = lax.axis_size(axis)
        ends = count - 1
        head = lax.slice_in_dim(cells, 0, width, axis=dim)
        tail = lax.slice_in_dim(cells, cells.shape[dim] - width, cells.shape[dim], axis=dim)
        cells = jnp.concatenate(
            [
                lax.ppermute(tail, axis, [(i, (i + 1) % count) for i in range(ends)]),
                cells,
                lax.ppermute(head, axis, [((i + 1) % count, i) for i in range(ends)]),
            ],
            axis=dim,
        )
    return cells


def unfold_taps(padded, rows_out, cols_out):
    taps = [
        padded[:, row_shift : row_shift + rows_out, col_shift : col_shift + cols_out, :]
        for row_shift in range(3)
        for col_shift in range(3)
    ]
    joined = jnp.concatenate(taps, axis=-1)
    return joined.reshape(-1, joined.shape[-1])


def convolve_local(padded_rows, weight, bias_vec, rows_out):
    images_here = padded_rows.shape[0]
    cols_out = padded_rows.shape[2]
    both_sides = jnp.pad(padded_rows, ((0, 0), (0, 0), (1, 1), (0, 0)))
    result = (
        jnp.dot(
            unfold_taps(both_sides, rows_out, cols_out), weight, preferred_element_type=jnp.float32
        )
        + bias_vec
    )
    return result.astype(jnp.bfloat16).reshape(images_here, rows_out, cols_out, weight.shape[1])


def group_stats(features):
    images_here = features.shape[0]
    channels = features.shape[3]
    grouped = features.astype(jnp.float32).reshape(images_here, -1, GROUPS, channels // GROUPS)
    cells_total = grouped.shape[1] * grouped.shape[3] * lax.axis_size("seq")
    sums_all = lax.psum(jnp.sum(grouped, axis=(1, 3)), "seq")
    centre = sums_all / cells_total
    deviate = grouped - centre[:, None, :, None]
    squares_all = lax.psum(jnp.sum(deviate * deviate, axis=(1, 3)), "seq")
    spread = squares_all / cells_total
    return (centre, spread)


def activate(features, centre, spread, norm_gain, norm_shift):
    images_here, rows_here, cols_here, channels = features.shape
    grouped = features.astype(jnp.float32).reshape(
        images_here, rows_here, cols_here, GROUPS, channels // GROUPS
    )
    normed = (grouped - centre[:, None, None, :, None]) / jnp.sqrt(
        spread[:, None, None, :, None] + 1e-06
    )
    normed = normed.reshape(images_here, rows_here, cols_here, channels) * norm_gain + norm_shift
    return jax.nn.silu(normed)


def on_device(
    conditioning,
    mod_weight,
    mod_bias,
    hidden,
    proj_weight,
    proj_bias,
    noisy_latent,
    in_weight,
    in_bias,
    norm_gain,
    norm_shift,
    conv_weight,
    conv_bias,
):
    gated = jax.nn.silu(conditioning.astype(jnp.float32)).astype(jnp.bfloat16)
    local_mod = (jnp.dot(gated, mod_weight, preferred_element_type=jnp.float32) + mod_bias).astype(
        jnp.bfloat16
    )
    modulation = lax.all_gather(local_mod, ("seq", "grp"), axis=1, tiled=True)
    images_here = hidden.shape[0]
    token_cols = hidden.shape[1]
    feature_dim = hidden.shape[2]
    own_rows = lax.dynamic_slice_in_dim(
        modulation, lax.axis_index("grp") * images_here, images_here, 0
    )
    scale_part = own_rows[:, :feature_dim].astype(jnp.float32)[:, None, :]
    shift_part = own_rows[:, feature_dim:].astype(jnp.float32)[:, None, :]
    values = hidden.astype(jnp.float32)
    centred = values - jnp.mean(values, axis=-1, keepdims=True)
    variance = jnp.mean(centred * centred, axis=-1, keepdims=True)
    modulated = (centred / jnp.sqrt(variance + 1e-06) * (1.0 + scale_part) + shift_part).astype(
        jnp.bfloat16
    )
    packed = (
        jnp.einsum("itd,dp->itp", modulated, proj_weight, preferred_element_type=jnp.float32)
        + proj_bias
    )
    lat_channels = proj_bias.shape[0] // 4
    velocity = packed.reshape(images_here, token_cols, lat_channels, 2, 2).transpose(0, 3, 1, 4, 2)
    velocity = velocity.reshape(images_here, 2, 2 * token_cols, lat_channels)
    latent = ((noisy_latent.astype(jnp.float32) - 0.75 * velocity) / 0.3611 + 0.1159).astype(
        jnp.bfloat16
    )
    padded = padded_2(latent, (("seq", 1),), 1)
    features = convolve_local(padded, in_weight, in_bias, 2)
    centre, spread = group_stats(features)
    activated = activate(features, centre, spread, norm_gain, norm_shift).astype(jnp.bfloat16)
    act_pad = padded_2(activated, (("seq", 1),), 1)
    cols_here = act_pad.shape[2]
    both_sides = jnp.pad(act_pad, ((0, 0), (0, 0), (1, 1), (0, 0)))
    columns = unfold_taps(both_sides, 2, cols_here)
    channels = conv_weight.shape[1]
    branch = jnp.dot(
        columns,
        lax.all_gather(conv_weight, "seq", axis=0, tiled=True),
        preferred_element_type=jnp.float32,
    )
    decoded = branch + conv_bias
    return decoded.astype(jnp.bfloat16).reshape(images_here, 2, cols_here, channels)


def solution(mesh):
    placed = (
        P(),
        P(None, ("seq", "grp")),
        P(("seq", "grp")),
        P("grp", "seq", None),
        P(),
        P(),
        P("grp", "seq", None, None),
        P(),
        P(),
        P(),
        P(),
        P("seq", None),
        P(),
    )
    return jax.shard_map(
        on_device,
        mesh=mesh,
        in_specs=placed,
        out_specs=P("grp", "seq", None, None),
        check_vma=False,
    )
```

profile of v0, /device:TPU:1, one launch (start us, length us, event | category | flops | bytes accessed | tf_op | source)
XLA Modules:
  0.0 1547.2 jit_solution(11177030963468075025)
XLA Ops:
  7.3 1.2 fusion.22
  8.5 1253.6 %all-gather = bf16[512,12,32]{2,1,0:T(8,128)(2,1)S(1)} all-gather(bf16[1,12,32]{2,1,0:T(8,128)(2,1)S(1)} %fusion.22), channel_id=1, replica_groups=mesh['seq'=64,'grp'=8] {'seq','grp'}, dimensions={0}, use_global_device_ids=true | all-gather | bytes 393984 | tf_op jit(solution)/shard_map/all_gather | solution.py:93
  1262.1 1.6 reshape.60
  1263.7 2.0 constant_dynamic-slice_fusion
  1265.7 1.3 copy.76
  1269.5 1.9 collective-permute-start
  1271.4 11.5 collective-permute-start.1
  1285.2 1.9 copy.72
  1287.0 3.2 reshape.58
  1290.2 2.0 reduce_sum.38
  1292.3 104.4 %psum.14 = f32[4,32]{1,0:T(4,128)S(1)} all-reduce(f32[4,32]{1,0:T(4,128)S(1)} %copy.73), channel_id=1, replica_groups=mesh['seq'=64,'grp'=8] {'seq'}, use_global_device_ids=true, to_apply=%region_3.4 | all-reduce | flops 128 | bytes 1024 | tf_op jit(solution)/shard_map/psum | solution.py:54
  1396.7 2.3 multiply_reduce_fusion
  1399.1 104.8 %psum.15 = f32[4,32]{1,0:T(4,128)S(1)} all-reduce(f32[4,32]{1,0:T(4,128)S(1)} %copy.75), channel_id=1, replica_groups=mesh['seq'=64,'grp'=8] {'seq'}, use_global_device_ids=true, to_apply=%region_5.6 | all-reduce | flops 128 | bytes 1024 | tf_op jit(solution)/shard_map/psum | solution.py:57
  1505.1 1.9 collective-permute-start.2
  1507.0 2.6 collective-permute-start.3
  1509.7 9.1 collective-permute-done.2
  1519.5 1.1 slice_dynamic-update-slice_fusion.5
  1520.6 1.2 fusion.24
  1521.8 1.2 slice_dynamic-update-slice_fusion.4
  1524.1 1.7 constant_dynamic-update-slice_fusion.9
  1525.8 1.3 slice_dynamic-update-slice_fusion.2
  1527.1 1.1 slice_dynamic-update-slice_fusion.1
  1529.3 1.3 slice_dynamic-update-slice_fusion
  1530.6 9.8 add_convert_fusion
  (65 shorter events, 9.5 us)
Async XLA Ops:
  6.5 1261.5 %copy-start = (bf16[3072,64]{0,1:T(8,128)(2,1)S(1)}, bf16[3072,64]{0,1:T(8,128)(2,1)}, u32[]{:S(2)}) copy-start(bf16[3072,64]{0,1:T(8,128)(2,1)} %param.17) | copy-start | bytes 1179652
  6.5 1524.1 %all-gather.3.cloned.1.call-start = ((), (), s32[]{:S(2)}) async-start(), calls=%async_computation | async-start | bytes 4792320 | tf_op jit(solution)/shard_map/all_gather | solution.py:129
  1263.7 3.4 copy-start.1
  1265.7 2.3 copy-start.9
  1267.1 0.9 copy-start.2
  1268.0 1.4 copy-start.4
  1268.9 15.8 %copy-start.3 = (bf16[144,512]{1,0:T(8,128)(2,1)S(1)}, bf16[144,512]{1,0:T(8,128)(2,1)}, u32[]{:S(2)}) copy-start(bf16[144,512]{1,0:T(8,128)(2,1)} %param.20) | copy-start | bytes 442372
  1268.9 15.8 %copy-start.7 = (f32[512]{0:T(512)S(1)}, f32[512]{0:T(512)}, u32[]{:S(2)}) copy-start(f32[512]{0:T(512)} %param.21) | copy-start | bytes 6148
  1269.5 13.4 collective-permute-start
  1271.4 12.3 collective-permute-start.1
  1290.2 214.1 %copy-start.5 = (f32[512]{0:T(512)S(1)}, f32[512]{0:T(512)}, u32[]{:S(2)}) copy-start(f32[512]{0:T(512)} %param.23) | copy-start | bytes 6148
  1290.2 214.1 %copy-start.6 = (f32[512]{0:T(512)S(1)}, f32[512]{0:T(512)}, u32[]{:S(2)}) copy-start(f32[512]{0:T(512)} %param.22) | copy-start | bytes 6148
  1505.1 13.7 collective-permute-start.2
  1507.0 11.7 collective-permute-start.3
  1528.2 2.4 copy-start.8
Sparse Core Ops, SparseCore 0:
  9.5 131.0 all-gather.2
where the time goes:
time: 1550 us
  blocking collectives  1460 us (94%)
  local copies, waits for them, and re-layouts  19.3 us (1%)
  starting transfers between devices  17.9 us (1%)
    all_gather x1, blocking collectives, on_device(): modulation = lax.all_gather(local_mod, ('seq', 'grp'), axis=1, tiled=True)  1250 us
    psum x1, blocking collectives, group_stats(): squares_all = lax.psum(jnp.sum(deviate * deviate, axis=(1, 3)), 'seq')  105 us
    psum x1, blocking collectives, group_stats(): sums_all = lax.psum(jnp.sum(grouped, axis=(1, 3)), 'seq')  104 us
  transfers between devices with their start and end apart: 5, of which 2 were waited for; matrix products, arithmetic and copies ran while one was open for 2% of the time, Pallas kernels for 0%

commit v1 on v0

v1 whole, which is shorter than its diff:
```python
import functools

import jax
import jax.numpy as jnp
import ml_dtypes
import numpy as np
from jax import lax
from jax.experimental import pallas as pl
from jax.experimental.pallas import tpu as pltpu
from jax.sharding import PartitionSpec as P

F32 = jnp.float32
BF16 = jnp.bfloat16
NT = (((1,), (1,)), ((), ()))
N_IMG = 4
COLS = 64
LANES = 128


def tables():
    taps = np.zeros((2, 2, 256, 144), np.float32)
    for odd in range(2):
        for low in range(2):
            for block in range(2):
                for down in range(2):
                    for k in range(16):
                        for i in range(2):
                            for j in range(2):
                                a = 2 * down + i - low
                                b = 2 * block + j + odd - 1
                                if 0 <= a <= 2 and 0 <= b <= 2:
                                    row = block * 128 + down * 64 + 4 * k + 2 * i + j
                                    taps[odd, low, row, (3 * a + b) * 16 + k] = 1
    split = np.zeros((128, 128), np.float32)
    for j in range(2):
        for c in range(64):
            split[j * 64 + c, 2 * c + j] = 1
    place = np.zeros((2, 4, 128, 128), np.float32)
    for j in range(2):
        for n in range(4):
            for i in range(2):
                for k in range(16):
                    for twin in range(2):
                        place[j, n, n * 32 + i * 16 + k, twin * 64 + 4 * k + 2 * i + j] = 1
    widen = np.zeros((512, 384), np.float32)
    for q in range(4):
        for l in range(96):
            widen[q * 128 + l, q * 96 + l] = 1
    channel = np.arange(512)
    same = (channel[:, None] // 16 == channel[None, :] // 16).astype(np.float32)
    spread = (np.arange(128)[:, None] % 32 == channel[None, :] // 16).astype(np.float32)
    kinds = (
        taps.reshape(1024, 144),
        split,
        place.reshape(1024, 128),
        widen,
        same,
        spread,
    )
    return [k.astype(ml_dtypes.bfloat16) for k in kinds]


def thirds(x):
    first = x.astype(BF16).astype(F32)
    rest = x - first
    second = rest.astype(BF16).astype(F32)
    third = rest - second
    return jnp.concatenate([first, second, third, jnp.zeros_like(x)], axis=0).astype(BF16)


def exact_dot(x, ones, dims):
    rows = x.shape[0]
    y = lax.dot_general(thirds(x), ones, dims, preferred_element_type=F32)
    return y[:rows] + y[rows : 2 * rows] + y[2 * rows : 3 * rows]


NN = (((1,), (0,)), ((), ()))


def kernel(
    nz,
    ngrp,
    cond_ref,
    modw_ref,
    modb_ref,
    hid_hbm,
    projw_ref,
    projb_ref,
    noisy_ref,
    inw_ref,
    inb_ref,
    gain_ref,
    shift_ref,
    convw_ref,
    convb_ref,
    taps_hbm,
    split_ref,
    place_ref,
    widen_ref,
    same_ref,
    spread_ref,
    out_ref,
    hid_ref,
    taps_ref,
    xn_ref,
    mod_ref,
    sc_ref,
    a1src,
    a1buf,
    a3buf,
    npk_ref,
    lat_ref,
    halo_ref,
    wb_ref,
    feat_ref,
    act_ref,
    c1buf,
    c2buf,
    stg_ref,
    rcv_ref,
    wbuf,
    ld_sem,
    sw_sem,
    a1_s,
    a1_r,
    a2_s,
    a2_r,
    a3_s,
    a3_r,
    b_s,
    b_r,
    c1_s,
    c1_r,
    c2_s,
    c2_r,
    zp_s,
    zp_r,
    zm_s,
    zm_r,
    y_s,
    y_r,
    k_s,
    k_r,
):
    nseq = 4 * nz
    s = lax.axis_index("seq")
    g = lax.axis_index("grp")
    z = lax.div(s, 4)
    q = lax.rem(s, 4)
    ylo = lax.div(q, 2)
    core = lax.rem(q, 2)
    x = lax.div(g, 2)
    yhi = lax.rem(g, 2)
    yy = 2 * yhi + ylo

    def at_z(zz):
        return {"seq": zz * 4 + q, "grp": g}

    def at_y(step):
        new = lax.rem(yy + 4 + step, 4)
        return {
            "seq": z * 4 + lax.rem(new, 2) * 2 + core,
            "grp": x * 2 + lax.div(new, 2),
        }

    def at_q(o):
        return {"seq": z * 4 + lax.rem(q + o, 4), "grp": g}

    def at_g(o):
        return {"seq": s, "grp": lax.rem(g + o, ngrp)}

    def at_s(step):
        return {"seq": lax.rem(s + nseq + step, nseq), "grp": g}

    mate = {"seq": z * 4 + ylo * 2 + (1 - core), "grp": g}

    def zmod(o):
        return lax.rem(z + nz + o, nz)

    pending = []

    def send(src, dst, ssem, rsem, where):
        copy = pltpu.make_async_remote_copy(
            src_ref=src,
            dst_ref=dst,
            send_sem=ssem,
            recv_sem=rsem,
            device_id=where,
            device_id_type=pl.DeviceIdType.MESH,
        )
        copy.start()
        pending.append(copy)
        return copy

    load_hid = pltpu.make_async_copy(hid_hbm, hid_ref, ld_sem.at[0])
    load_hid.start()
    load_taps = pltpu.make_async_copy(taps_hbm, taps_ref, ld_sem.at[1])
    load_taps.start()

    barrier = pltpu.get_barrier_semaphore()
    greeted = (
        [at_z(zmod(o)) for o in range(1, nz)]
        + [at_g(o) for o in range(1, ngrp)]
        + [at_q(o) for o in range(1, 4)]
        + [at_y(1), at_y(-1), at_s(1), at_s(-1), mate]
    )
    for where in greeted:
        pl.semaphore_signal(barrier, inc=1, device_id=where, device_id_type=pl.DeviceIdType.MESH)

    rows = convw_ref.shape[0]
    whole = convw_ref[...].astype(F32)
    stg_ref[0] = whole[:, :256]
    stg_ref[1] = whole[:, 256:]
    v = cond_ref[...].astype(F32)
    gated = (v / (1.0 + jnp.exp(-v))).astype(BF16)
    own_mod = lax.dot_general(gated, modw_ref[...], NT, preferred_element_type=F32) + modb_ref[...]
    mcols = own_mod.shape[1]
    spot = lax.broadcasted_iota(jnp.int32, (mcols, LANES), 0) + g * mcols
    lane = lax.broadcasted_iota(jnp.int32, (mcols, LANES), 1)
    put = jnp.where(spot == lane, 1.0, 0.0).astype(BF16)
    placed = jnp.dot(own_mod.astype(BF16), put, preferred_element_type=F32)
    for o in range(ngrp):
        a1src[o] = placed[N_IMG * o : N_IMG * (o + 1)]

    pl.semaphore_wait(barrier, len(greeted))

    swap = send(stg_ref.at[1 - core], rcv_ref, sw_sem.at[0], sw_sem.at[1], mate)
    a1 = []
    for o in range(1, ngrp):
        peer = at_g(o)
        a1.append(
            send(a1src.at[peer["grp"]], a1buf.at[o], a1_s.at[o - 1], a1_r.at[o - 1], peer)
        )

    def chunk(zz, half_y):
        return pl.ds(pl.multiple_of((2 * zz + half_y) * (2 * rows), 16), 2 * rows)

    swap.wait_recv()
    here = stg_ref[core]
    there = rcv_ref[...]
    top = jnp.where(core == 0, here, there)
    bottom = jnp.where(core == 0, there, here)
    wbuf[core, chunk(z, ylo), :] = jnp.concatenate([top, bottom], axis=0).astype(BF16)

    n_plus, n_minus = nz // 2, nz // 2 - 1
    zp, zm, ycopies, kcopies = {}, {}, {}, []

    def spread_chunk(slot, zz):
        at = chunk(zz, ylo)
        ycopies[slot] = [
            send(
                wbuf.at[core, at, pl.ds(0, 128)],
                wbuf.at[core, at, pl.ds(0, 128)],
                y_s.at[slot, 0],
                y_r.at[slot, 0],
                at_y(1),
            ),
            send(
                wbuf.at[core, at, pl.ds(128, 128)],
                wbuf.at[core, at, pl.ds(128, 128)],
                y_s.at[slot, 1],
                y_r.at[slot, 1],
                at_y(-1),
            ),
        ]
        kcopies.append(
            send(wbuf.at[core, at], wbuf.at[core, at], k_s.at[slot, 0], k_r.at[slot, 0], mate)
        )

    def pass_y(slot, zz):
        for copy in ycopies[slot]:
            copy.wait_recv()
        at = chunk(zz, 1 - ylo)
        kcopies.append(
            send(wbuf.at[core, at], wbuf.at[core, at], k_s.at[slot, 1], k_r.at[slot, 1], mate)
        )

    def slots(k):
        if k == 0:
            return [(0, zmod(0))]
        out = []
        if k <= n_plus:
            out.append((2 * k - 1, zmod(-k)))
        if k <= n_minus:
            out.append((2 * k, zmod(k)))
        return out

    def tick(k):
        if 1 <= k <= n_plus:
            zp[k].wait_recv()
        if k < n_plus:
            at = chunk(zmod(-k), ylo)
            zp[k + 1] = send(
                wbuf.at[core, at], wbuf.at[core, at], zp_s.at[k], zp_r.at[k], at_z(zmod(1))
            )
        if 1 <= k <= n_minus:
            zm[k].wait_recv()
        if k < n_minus:
            at = chunk(zmod(k), ylo)
            zm[k + 1] = send(
                wbuf.at[core, at], wbuf.at[core, at], zm_s.at[k], zm_r.at[k], at_z(zmod(-1))
            )
        if k <= n_plus:
            for slot, zz in slots(k):
                spread_chunk(slot, zz)
        if 1 <= k <= n_plus + 1:
            for slot, zz in slots(k - 1):
                pass_y(slot, zz)

    last_tick = n_plus + 1
    clock = [0]

    def next_tick():
        if clock[0] <= last_tick:
            tick(clock[0])
            clock[0] += 1

    next_tick()

    for copy in a1:
        copy.wait_recv()
    merged = a1src[g]
    for o in range(1, ngrp):
        merged = merged + a1buf[o]
    a3buf[q, z] = merged
    a2 = []
    for o in range(1, nz):
        a2.append(
            send(a3buf.at[q, z], a3buf.at[q, z], a2_s.at[o - 1], a2_r.at[o - 1], at_z(zmod(o)))
        )

    load_hid.wait()

    def norm_rows(first, count):
        def body(step, carry):
            at = pl.ds(pl.multiple_of(step * 16, 16), 16)
            h = hid_ref[at, :].astype(F32)
            c = h - jnp.mean(h, axis=-1, keepdims=True)
            var = jnp.mean(c * c, axis=-1, keepdims=True)
            xn_ref[at, :] = c * lax.rsqrt(var + 1e-06)
            return carry

        lax.fori_loop(first, first + count, body, 0)

    norm_rows(0, 8)
    next_tick()
    for copy in a2:
        copy.wait_recv()
    a3 = []
    for o in range(1, 4):
        a3.append(send(a3buf.at[q], a3buf.at[q], a3_s.at[o - 1], a3_r.at[o - 1], at_q(o)))
    norm_rows(8, 8)

    de = lax.dot_general(split_ref[...], noisy_ref[...], NT, preferred_element_type=F32).astype(BF16)
    for n in range(N_IMG):
        npk_ref[pl.ds(n * COLS, COLS), :] = jnp.dot(
            de[:64], place_ref[pl.ds(n * 128, 128), :], preferred_element_type=F32
        ) + jnp.dot(de[64:], place_ref[pl.ds(512 + n * 128, 128), :], preferred_element_type=F32)
    next_tick()
    load_taps.wait()
    for odd in range(2):
        for low in range(2):
            wb_ref[odd, :, pl.ds(512 * low, 512)] = jnp.dot(
                taps_ref[pl.ds((2 * odd + low) * 256, 256), :],
                inw_ref[...],
                preferred_element_type=F32,
            ).astype(BF16)

    for copy in a3:
        copy.wait_recv()
    for qq in range(4):
        for zz in range(nz):
            sc_ref[pl.ds(N_IMG * zz, N_IMG), pl.ds(LANES * qq, LANES)] = a3buf[qq, zz]
    table = jnp.dot(sc_ref[...].astype(BF16), widen_ref[...], preferred_element_type=F32)
    half = nz // 2
    for n in range(N_IMG):
        for zz in range(half):
            at = (pl.ds(n * COLS, COLS), pl.ds(384 * zz, 384))
            lift = table[N_IMG * zz + n : N_IMG * zz + n + 1]
            move = table[N_IMG * (zz + half) + n : N_IMG * (zz + half) + n + 1]
            mod_ref[at] = (xn_ref[at] * (1.0 + lift) + move).astype(BF16)
    proj = projw_ref[...]
    packed = lax.dot_general(
        mod_ref[...], jnp.concatenate([proj, proj], axis=0), NT, preferred_element_type=F32
    )
    packed = packed + projb_ref[...]
    lat_ref[...] = ((npk_ref[...] - 0.75 * packed) / 0.3611 + 0.1159).astype(BF16)
    down = send(lat_ref, halo_ref.at[0], b_s.at[0], b_r.at[0], at_s(1))
    up = send(lat_ref, halo_ref.at[1], b_s.at[1], b_r.at[1], at_s(-1))
    next_tick()

    down.wait_recv()
    up.wait_recv()
    lat = lat_ref[...].astype(F32)
    above = jnp.where(s == 0, 0.0, halo_ref[0].astype(F32))
    below = jnp.where(s == nseq - 1, 0.0, halo_ref[1].astype(F32))
    left = lax.broadcasted_iota(jnp.int32, (N_IMG * COLS, LANES), 1) < 64
    column = lax.rem(lax.broadcasted_iota(jnp.int32, (N_IMG * COLS, LANES), 0), COLS)
    for pair in range(2):
        both = jnp.where(left, above, lat) if pair == 0 else jnp.where(left, lat, below)
        before = jnp.where(column == 0, 0.0, pltpu.roll(both, 1, 0))
        after = jnp.where(column == COLS - 1, 0.0, pltpu.roll(both, N_IMG * COLS - 1, 0))
        for odd in range(2):
            parts = [before, both] if odd == 0 else [both, after]
            patch = jnp.concatenate(parts, axis=1).astype(BF16)
            for low in range(2):
                feat_ref[2 * pair + low, odd] = (
                    jnp.dot(
                        patch, wb_ref[odd, :, pl.ds(512 * low, 512)], preferred_element_type=F32
                    )
                    + inb_ref[...]
                ).astype(BF16)
    next_tick()

    own = [(1, 0), (1, 1), (2, 0), (2, 1)]
    means, moments = [], []
    for n in range(N_IMG):
        at = pl.ds(n * COLS, COLS)
        total = jnp.zeros((1, 512), F32)
        for h, odd in own:
            total = total + jnp.sum(feat_ref[h, odd, at, :].astype(F32), axis=0, keepdims=True)
        mean = total / 256.0
        moment = jnp.zeros((1, 512), F32)
        for h, odd in own:
            d = feat_ref[h, odd, at, :].astype(F32) - mean
            moment = moment + jnp.sum(d * d, axis=0, keepdims=True)
        means.append(mean)
        moments.append(moment)
    empty = jnp.zeros((4, 512), F32)
    mean4 = jnp.concatenate(means + [empty], axis=0)
    moment4 = jnp.concatenate(moments + [empty], axis=0)
    group = exact_dot(mean4, same_ref[...], NN) / 16.0
    gap = mean4 - group
    moment4 = moment4 + 256.0 * gap * gap
    packed8 = exact_dot(
        jnp.concatenate([mean4[:4], moment4[:4]], axis=0), spread_ref[...], NT
    )
    row8 = lax.broadcasted_iota(jnp.int32, (8, LANES), 0)
    lane8 = lax.broadcasted_iota(jnp.int32, (8, LANES), 1)
    mine = lax.rem(row8, 4) == lax.div(lane8, 32)
    packed8 = jnp.where(mine, packed8, 0.0)
    c1buf[q, 0:1] = jnp.sum(packed8[:4], axis=0, keepdims=True) / 16.0
    c1buf[q, 1:2] = jnp.sum(packed8[4:], axis=0, keepdims=True)
    c1 = []
    for o in range(1, 4):
        c1.append(send(c1buf.at[q], c1buf.at[q], c1_s.at[o - 1], c1_r.at[o - 1], at_q(o)))
    next_tick()
    for copy in c1:
        copy.wait_recv()

    def merge(buf, count, each):
        centre = buf[0, 0:1]
        for o in range(1, count):
            centre = centre + buf[o, 0:1]
        centre = centre / count
        square = jnp.zeros_like(centre)
        for o in range(count):
            d = buf[o, 0:1] - centre
            square = square + buf[o, 1:2] + each * (d * d)
        return centre, square

    centre, square = merge(c1buf, 4, 4096.0)
    c2buf[z, 0:1] = centre
    c2buf[z, 1:2] = square
    c2 = []
    for o in range(1, nz):
        c2.append(
            send(c2buf.at[z], c2buf.at[z], c2_s.at[o - 1], c2_r.at[o - 1], at_z(zmod(o)))
        )
    next_tick()
    for copy in c2:
        copy.wait_recv()
    centre, square = merge(c2buf, nz, 4.0 * 4096.0)
    rate = lax.rsqrt(square / (4096.0 * nseq) + 1e-06)
    both8 = jnp.where(mine, jnp.where(row8 < 4, centre, rate), 0.0)
    wide = exact_dot(both8, spread_ref[...], NN)

    next_tick()
    first_row = lax.broadcasted_iota(jnp.int32, (COLS, 512), 0)
    keep_top = jnp.where(s == 0, 0.0, 1.0)
    keep_bottom = jnp.where(s == nseq - 1, 0.0, 1.0)
    for n in range(N_IMG):
        at = pl.ds(n * COLS, COLS)
        cen = wide[n : n + 1]
        slope = wide[4 + n : 5 + n] * gain_ref[...]
        for h in range(4):
            for odd in range(2):
                t = (feat_ref[h, odd, at, :].astype(F32) - cen) * slope + shift_ref[...]
                t = 0.5 * t
                act = t + t * jnp.tanh(t)
                if h == 0:
                    act = act * keep_top
                if h == 3:
                    act = act * keep_bottom
                act_ref[h, 1 + odd, at, :] = act.astype(BF16)
                if odd == 0:
                    moved = jnp.where(first_row == COLS - 1, 0.0, pltpu.roll(act, COLS - 1, 0))
                    act_ref[h, 3, at, :] = moved.astype(BF16)
                else:
                    moved = jnp.where(first_row == 0, 0.0, pltpu.roll(act, 1, 0))
                    act_ref[h, 0, at, :] = moved.astype(BF16)
    while clock[0] <= last_tick:
        next_tick()
    for copy in kcopies:
        copy.wait_recv()

    for rho in range(2):
        for part in range(2):
            acc = None
            for a in range(3):
                for b in range(3):
                    lhs = act_ref[rho + a, pl.ds(b, 2)].reshape(2 * N_IMG * COLS, 512)
                    term = jnp.dot(
                        lhs,
                        wbuf[part, pl.ds((3 * a + b) * 512, 512), :],
                        preferred_element_type=F32,
                    )
                    acc = term if acc is None else acc + term
            acc = (acc + convb_ref[:, pl.ds(256 * part, 256)]).astype(BF16)
            for odd in range(2):
                for n in range(N_IMG):
                    first = (odd * N_IMG + n) * COLS
                    out_ref[n, rho, :, pl.ds(512 * odd + 256 * part, 256)] = acc[
                        first : first + COLS
                    ]
    for copy in pending:
        copy.wait_send()


def on_device(
    nz,
    ngrp,
    conditioning,
    mod_weight,
    mod_bias,
    hidden,
    proj_weight,
    proj_bias,
    noisy_latent,
    in_weight,
    in_bias,
    norm_gain,
    norm_shift,
    conv_weight,
    conv_bias,
):
    width = hidden.shape[2]
    tokens = N_IMG * COLS
    shard = conv_weight.shape[0]
    vmem = pl.BlockSpec(memory_space=pltpu.VMEM)
    hbm = pl.BlockSpec(memory_space=pl.ANY)
    dma = pltpu.SemaphoreType.DMA
    n_plus = nz // 2
    consts = [jnp.asarray(t) for t in tables()]
    scratch = [
        pltpu.VMEM((tokens, width), BF16),
        pltpu.VMEM((1024, 144), BF16),
        pltpu.VMEM((tokens, width), F32),
        pltpu.VMEM((tokens, width), BF16),
        pltpu.VMEM((N_IMG * nz, 512), F32),
        pltpu.VMEM((ngrp, N_IMG, LANES), F32),
        pltpu.VMEM((ngrp, N_IMG, LANES), F32),
        pltpu.VMEM((4, nz, N_IMG, LANES), F32),
        pltpu.VMEM((tokens, LANES), F32),
        pltpu.VMEM((tokens, LANES), BF16),
        pltpu.VMEM((2, tokens, LANES), BF16),
        pltpu.VMEM((2, 256, 1024), BF16),
        pltpu.VMEM((4, 2, tokens, 512), BF16),
        pltpu.VMEM((4, 4, tokens, 512), BF16),
        pltpu.VMEM((4, 2, LANES), F32),
        pltpu.VMEM((nz, 2, LANES), F32),
        pltpu.VMEM((2, shard, 256), F32),
        pltpu.VMEM((shard, 256), F32),
        pltpu.VMEM((2, shard * 4 * nz, 256), BF16),
        dma((2,)),
        dma((2,)),
        dma((ngrp - 1,)),
        dma((ngrp - 1,)),
        dma((nz - 1,)),
        dma((nz - 1,)),
        dma((3,)),
        dma((3,)),
        dma((2,)),
        dma((2,)),
        dma((3,)),
        dma((3,)),
        dma((nz - 1,)),
        dma((nz - 1,)),
        dma((n_plus,)),
        dma((n_plus,)),
        dma((n_plus,)),
        dma((n_plus,)),
        dma((nz, 2)),
        dma((nz, 2)),
        dma((nz, 2)),
        dma((nz, 2)),
    ]
    out = pl.pallas_call(
        functools.partial(kernel, nz, ngrp),
        out_shape=jax.ShapeDtypeStruct((N_IMG, 2, COLS, 1024), BF16),
        in_specs=[vmem] * 3 + [hbm] + [vmem] * 9 + [hbm] + [vmem] * 5,
        out_specs=vmem,
        scratch_shapes=scratch,
        compiler_params=pltpu.CompilerParams(
            collective_id=0, has_side_effects=True, vmem_limit_bytes=56 * 1024 * 1024
        ),
    )(
        conditioning,
        mod_weight.T,
        mod_bias.reshape(1, -1),
        hidden.reshape(tokens, width),
        proj_weight.T,
        jnp.concatenate([proj_bias, proj_bias]).reshape(1, -1),
        noisy_latent.transpose(0, 1, 3, 2).reshape(128, 128),
        in_weight,
        in_bias.reshape(1, -1),
        norm_gain.reshape(1, -1),
        norm_shift.reshape(1, -1),
        conv_weight,
        conv_bias.reshape(1, -1),
        *consts,
    )
    return out.reshape(N_IMG, 2, 2 * COLS, 512)


def solution(mesh):
    nz = mesh.shape["seq"] // 4
    ngrp = mesh.shape["grp"]
    placed = (
        P(),
        P(None, ("seq", "grp")),
        P(("seq", "grp")),
        P("grp", "seq", None),
        P(),
        P(),
        P("grp", "seq", None, None),
        P(),
        P(),
        P(),
        P(),
        P("seq", None),
        P(),
    )
    return jax.shard_map(
        functools.partial(on_device, nz, ngrp),
        mesh=mesh,
        in_specs=placed,
        out_specs=P("grp", "seq", None, None),
        check_vma=False,
    )
```

time: 1550 us -> 74 us (0.05)
  blocking collectives: 1460 us -> 0 us
  Pallas kernels: 0 us -> 70.3 us
  starting transfers between devices: 17.9 us -> 0 us
  local copies, waits for them, and re-layouts: 19.3 us -> 2.2 us
    all_gather x1 -> x0, blocking collectives: 1250 us -> none  [on_device(): modulation = lax.all_gather(local_mod, ('seq', 'grp'), axis=1, tiled=True)]
    psum x2 -> x0, blocking collectives: 209 us -> none  [the longest x1 105 us: group_stats(): squares_all = lax.psum(jnp.sum(deviate * deviate, axis=(1, 3)), 'seq')]
    pallas_call x0 -> x1, Pallas kernels: none -> 70.3 us  [on_device(): pl.pallas_call(functools.partial(kernel, nz, ngrp), out_shape=jax.ShapeDt...]
    ppermute x4 -> x0, starting transfers between devices: 17.9 us -> none  [the longest x2 14.1 us: padded_2(): lax.ppermute(head, axis, [((i + 1) % count, i) for i in range(ends)])]
  transfers between devices with their start and end apart: 5 -> 0, of which waited for: 2 -> 0; matrix products, arithmetic and copies ran while one was open for 2% -> 0% of each run, Pallas kernels for 0% -> 0%
where the time goes in v1:
time: 74 us; the launch traced here: 73.8 us
  Pallas kernels  70.3 us (95%)
  local copies, waits for them, and re-layouts  2.2 us (3%)
  other arithmetic  1.31 us (2%)
    pallas_call x1, Pallas kernels, on_device(): pl.pallas_call(functools.partial(kernel, nz, ngrp), out_shape=jax.ShapeDt...  70.3 us
    reshape x1, local copies, waits for them, and re-layouts, on_device(): return out.reshape(N_IMG, 2, 2 * COLS, 512)  2.2 us

profile of v1, /device:TPU:1, one launch (start us, length us, event | category | flops | bytes accessed | tf_op | source)
XLA Modules:
  0.0 73.8 jit_solution(7637985567895144953)
XLA Ops:
  0.0 1.3 %maximum_bitcast_fusion.projb_ref = f32[1,128]{1,0:T(1,128)} fusion(f32[64]{0:T(128)} %param.24), kind=kLoop, calls=%fused_computation | loop fusion | flops 128 | bytes 768 | tf_op jit(solution)/shard_map/reshape | solution.py:613
  1.3 70.3 %shard_map.181 = bf16[4,2,64,1024]{3,2,1,0:T(8,128)(2,1)} custom-call(bf16[32,3072]{1,0:T(8,128)(2,1)} %cond_ref.1, bf16[12,3072]{1,0:T(8,128)(2,1)} %bitcast.17, f32[1,12]{1,0:T(1,128)} %bitcast.23, bf16[256,3072]{1,0:T(8,128)(2,1)} %bitcast.15, bf16[64,3072]{1,0:T(8,128)(2,1)} %bitcast.16, f32[1,128]{1,0:T(1,128)} %maximum_bitcast_fusion.projb_ref, ...), custom_call_target="tpu_custom_call" | custom-call | tf_op jit(solution)/shard_map/pallas_call | solution.py:598
  71.6 2.2 %reshape.35 = bf16[4,2,128,512]{3,2,1,0:T(8,128)(2,1)} reshape(bf16[4,2,64,1024]{3,2,1,0:T(8,128)(2,1)} %shard_map.181) | data formatting | bytes 2097152 | tf_op jit(solution)/shard_map/reshape | solution.py:623

commit v2 on v1

--- a/solution.py
+++ b/solution.py
@@ -80,34 +80,45 @@
 def kernel(
     nz,
     ngrp,
-    cond_ref,
-    modw_ref,
+    cond_hbm,
+    modw_hbm,
     modb_ref,
     hid_hbm,
-    projw_ref,
+    projw_hbm,
     projb_ref,
-    noisy_ref,
-    inw_ref,
+    noisy_hbm,
+    inw_hbm,
     inb_ref,
     gain_ref,
     shift_ref,
-    convw_ref,
+    convw_hbm,
     convb_ref,
     taps_hbm,
+    split_hbm,
+    place_hbm,
+    widen_hbm,
+    same_hbm,
+    spread_hbm,
+    out_ref,
+    cond_ref,
+    modw_ref,
+    hid_ref,
+    projw_ref,
+    noisy_ref,
+    inw_ref,
+    convw_ref,
+    taps_ref,
     split_ref,
     place_ref,
     widen_ref,
     same_ref,
     spread_ref,
-    out_ref,
-    hid_ref,
-    taps_ref,
     xn_ref,
     mod_ref,
     sc_ref,
     a1src,
     a1buf,
-    a3buf,
+    a2buf,
     npk_ref,
     lat_ref,
     halo_ref,
@@ -125,18 +136,16 @@
     a1_r,
     a2_s,
     a2_r,
-    a3_s,
-    a3_r,
     b_s,
     b_r,
     c1_s,
     c1_r,
     c2_s,
     c2_r,
-    zp_s,
-    zp_r,
-    zm_s,
-    zm_r,
+    z_s,
+    z_r,
+    x_s,
+    x_r,
     y_s,
     y_r,
     k_s,
@@ -192,21 +201,45 @@
         pending.append(copy)
         return copy
 
-    load_hid = pltpu.make_async_copy(hid_hbm, hid_ref, ld_sem.at[0])
-    load_hid.start()
-    load_taps = pltpu.make_async_copy(taps_hbm, taps_ref, ld_sem.at[1])
-    load_taps.start()
-
+    def at_x(m):
+        return {"seq": s, "grp": lax.rem(x + m, ngrp // 2) * 2 + yhi}
+
+    def at_plane(oq, og):
+        return {"seq": z * 4 + lax.rem(q + oq, 4), "grp": lax.rem(g + og, ngrp)}
+
+    plane = [(oq, og) for oq in range(4) for og in range(ngrp) if oq or og]
     barrier = pltpu.get_barrier_semaphore()
     greeted = (
-        [at_z(zmod(o)) for o in range(1, nz)]
-        + [at_g(o) for o in range(1, ngrp)]
-        + [at_q(o) for o in range(1, 4)]
-        + [at_y(1), at_y(-1), at_s(1), at_s(-1), mate]
+        [at_z(zmod(o)) for o in sorted(range(1, nz), key=lambda o: -min(o, nz - o))]
+        + [at_plane(oq, og) for oq, og in plane]
+        + [at_s(1), at_s(-1)]
     )
     for where in greeted:
         pl.semaphore_signal(barrier, inc=1, device_id=where, device_id_type=pl.DeviceIdType.MESH)
 
+    loads = []
+    for i, (src, dst) in enumerate(
+        (
+            (convw_hbm, convw_ref),
+            (cond_hbm, cond_ref),
+            (modw_hbm, modw_ref),
+            (hid_hbm, hid_ref),
+            (noisy_hbm, noisy_ref),
+            (split_hbm, split_ref),
+            (place_hbm, place_ref),
+            (inw_hbm, inw_ref),
+            (taps_hbm, taps_ref),
+            (projw_hbm, projw_ref),
+            (widen_hbm, widen_ref),
+            (same_hbm, same_ref),
+            (spread_hbm, spread_ref),
+        )
+    ):
+        loads.append(pltpu.make_async_copy(src, dst, ld_sem.at[i]))
+        loads[-1].start()
+
+    for copy in loads[:3]:
+        copy.wait()
     rows = convw_ref.shape[0]
     whole = convw_ref[...].astype(F32)
     stg_ref[0] = whole[:, :256]
@@ -226,11 +259,9 @@
 
     swap = send(stg_ref.at[1 - core], rcv_ref, sw_sem.at[0], sw_sem.at[1], mate)
     a1 = []
-    for o in range(1, ngrp):
-        peer = at_g(o)
-        a1.append(
-            send(a1src.at[peer["grp"]], a1buf.at[o], a1_s.at[o - 1], a1_r.at[o - 1], peer)
-        )
+    for i, (oq, og) in enumerate(plane):
+        peer = at_plane(oq, og)
+        a1.append(send(a1src.at[peer["grp"]], a1buf.at[q, og], a1_s.at[i], a1_r.at[i], peer))
 
     def chunk(zz, half_y):
         return pl.ds(pl.multiple_of((2 * zz + half_y) * (2 * rows), 16), 2 * rows)
@@ -242,94 +273,167 @@
     bottom = jnp.where(core == 0, there, here)
     wbuf[core, chunk(z, ylo), :] = jnp.concatenate([top, bottom], axis=0).astype(BF16)
 
-    n_plus, n_minus = nz // 2, nz // 2 - 1
-    zp, zm, ycopies, kcopies = {}, {}, {}, []
-
-    def spread_chunk(slot, zz):
-        at = chunk(zz, ylo)
-        ycopies[slot] = [
-            send(
-                wbuf.at[core, at, pl.ds(0, 128)],
-                wbuf.at[core, at, pl.ds(0, 128)],
-                y_s.at[slot, 0],
-                y_r.at[slot, 0],
-                at_y(1),
-            ),
-            send(
-                wbuf.at[core, at, pl.ds(128, 128)],
-                wbuf.at[core, at, pl.ds(128, 128)],
-                y_s.at[slot, 1],
-                y_r.at[slot, 1],
-                at_y(-1),
-            ),
+    nx = ngrp // 2
+
+    def wanted(j, xx):
+        if nx == 1:
+            return j
+        quarter = nz // 4
+        near = [xx, nz // 2 - xx, nz // 2 + xx, nz - xx][j]
+        return jnp.where(xx == 0, quarter * j, near)
+
+    def guarded(j, xx, act):
+        if j == 0:
+            pl.when(xx > 0)(act)
+        else:
+            act()
+
+    per = nz if nx == 1 else 4
+    first, second = ([1], [0]) if nx == 1 else ([0, 3], [1, 2])
+
+    def copy_of(src, dst, ssem, rsem, where):
+        return pltpu.make_async_remote_copy(
+            src_ref=src,
+            dst_ref=dst,
+            send_sem=ssem,
+            recv_sem=rsem,
+            device_id=where,
+            device_id_type=pl.DeviceIdType.MESH,
+        )
+
+    def z_copy(j):
+        at = wbuf.at[core, chunk(z, ylo)]
+        return copy_of(at, at, z_s.at[j], z_r.at[j], at_z(lax.rem(z + nz - wanted(j, x), nz)))
+
+    def x_copy(m, j):
+        at = wbuf.at[core, chunk(lax.rem(z + wanted(j, x), nz), ylo)]
+        return copy_of(at, at, x_s.at[m, j], x_r.at[m, j], at_x(m))
+
+    def zz_of(m, j):
+        return lax.rem(z + wanted(j, lax.rem(x + nx - m, nx)), nz)
+
+    def y_copies(slot, zz):
+        at = wbuf.at[core, chunk(zz, ylo)]
+        return [
+            copy_of(
+                at.at[:, pl.ds(128 * i, 128)],
+                at.at[:, pl.ds(128 * i, 128)],
+                y_s.at[slot, i],
+                y_r.at[slot, i],
+                at_y(1 - 2 * i),
+            )
+            for i in range(2)
         ]
-        kcopies.append(
-            send(wbuf.at[core, at], wbuf.at[core, at], k_s.at[slot, 0], k_r.at[slot, 0], mate)
-        )
-
-    def pass_y(slot, zz):
-        for copy in ycopies[slot]:
+
+    def k_copy(slot, zz, other):
+        at = wbuf.at[core, chunk(zz, 1 - ylo if other else ylo)]
+        return copy_of(at, at, k_s.at[slot, other], k_r.at[slot, other], mate)
+
+    own_slot = nx * per
+    every = [(m, j) for m in range(nx) for j in range(per)]
+
+    def origin(m):
+        return lax.rem(x + nx - m, nx)
+
+    def start_own():
+        for j in range(per):
+            guarded(j, x, lambda j=j: z_copy(j).start())
+        for copy in y_copies(own_slot, z):
+            copy.start()
+        k_copy(own_slot, z, 0).start()
+
+    def onward(m, j):
+        for copy in y_copies(m * per + j, zz_of(m, j)):
+            copy.start()
+        k_copy(m * per + j, zz_of(m, j), 0).start()
+
+    def take_z(js):
+        for j in js:
+
+            def act(j=j):
+                z_copy(j).wait_recv()
+                for m in range(1, nx):
+                    x_copy(m, j).start()
+                onward(0, j)
+
+            guarded(j, x, act)
+
+    def take_x(js):
+        for m in range(1, nx):
+            for j in js:
+
+                def act(m=m, j=j):
+                    x_copy(m, j).wait_recv()
+                    onward(m, j)
+
+                guarded(j, origin(m), act)
+
+    def take_y_slot(slot, zz):
+        for copy in y_copies(slot, zz):
             copy.wait_recv()
-        at = chunk(zz, 1 - ylo)
-        kcopies.append(
-            send(wbuf.at[core, at], wbuf.at[core, at], k_s.at[slot, 1], k_r.at[slot, 1], mate)
-        )
-
-    def slots(k):
-        if k == 0:
-            return [(0, zmod(0))]
-        out = []
-        if k <= n_plus:
-            out.append((2 * k - 1, zmod(-k)))
-        if k <= n_minus:
-            out.append((2 * k, zmod(k)))
-        return out
-
-    def tick(k):
-        if 1 <= k <= n_plus:
-            zp[k].wait_recv()
-        if k < n_plus:
-            at = chunk(zmod(-k), ylo)
-            zp[k + 1] = send(
-                wbuf.at[core, at], wbuf.at[core, at], zp_s.at[k], zp_r.at[k], at_z(zmod(1))
-            )
-        if 1 <= k <= n_minus:
-            zm[k].wait_recv()
-        if k < n_minus:
-            at = chunk(zmod(k), ylo)
-            zm[k + 1] = send(
-                wbuf.at[core, at], wbuf.at[core, at], zm_s.at[k], zm_r.at[k], at_z(zmod(-1))
-            )
-        if k <= n_plus:
-            for slot, zz in slots(k):
-                spread_chunk(slot, zz)
-        if 1 <= k <= n_plus + 1:
-            for slot, zz in slots(k - 1):
-                pass_y(slot, zz)
-
-    last_tick = n_plus + 1
-    clock = [0]
-
-    def next_tick():
-        if clock[0] <= last_tick:
-            tick(clock[0])
-            clock[0] += 1
-
-    next_tick()
+        k_copy(slot, zz, 1).start()
+
+    def take_y(js):
+        for m in range(nx):
+            for j in js:
+                guarded(j, origin(m), lambda m=m, j=j: take_y_slot(m * per + j, zz_of(m, j)))
+
+    def finish_gather():
+        for other in range(2):
+            k_copy(own_slot, z, other).wait_recv()
+            for m, j in every:
+                guarded(
+                    j,
+                    origin(m),
+                    lambda m=m, j=j: k_copy(m * per + j, zz_of(m, j), other).wait_recv(),
+                )
+
+    def drain():
+        for j in range(per):
+
+            def sent(j=j):
+                z_copy(j).wait_send()
+                for m in range(1, nx):
+                    x_copy(m, j).wait_send()
+
+            guarded(j, x, sent)
+        for copy in y_copies(own_slot, z):
+            copy.wait_send()
+        for other in range(2):
+            k_copy(own_slot, z, other).wait_send()
+        for m, j in every:
+
+            def sent(m=m, j=j):
+                for copy in y_copies(m * per + j, zz_of(m, j)):
+                    copy.wait_send()
+                for other in range(2):
+                    k_copy(m * per + j, zz_of(m, j), other).wait_send()
+
+            guarded(j, origin(m), sent)
+
+    start_own()
 
     for copy in a1:
         copy.wait_recv()
-    merged = a1src[g]
-    for o in range(1, ngrp):
-        merged = merged + a1buf[o]
-    a3buf[q, z] = merged
+    pieces = []
+    for qq in range(4):
+        piece = jnp.where(q == qq, a1src[g], jnp.zeros((N_IMG, LANES), F32))
+        for og in range(ngrp):
+            block = a1buf[qq, og]
+            if og == 0:
+                block = jnp.where(q == qq, 0.0, block)
+            piece = piece + block
+        pieces.append(piece)
+    a2buf[z] = jnp.concatenate(pieces, axis=0).astype(BF16)
     a2 = []
-    for o in range(1, nz):
+    for o in sorted(range(1, nz), key=lambda o: -min(o, nz - o)):
         a2.append(
-            send(a3buf.at[q, z], a3buf.at[q, z], a2_s.at[o - 1], a2_r.at[o - 1], at_z(zmod(o)))
+            send(a2buf.at[z], a2buf.at[z], a2_s.at[o - 1], a2_r.at[o - 1], at_z(zmod(o)))
         )
 
-    load_hid.wait()
+    take_z(first)
+    for copy in loads[3:]:
+        copy.wait()
 
     def norm_rows(first, count):
         def body(step, carry):
@@ -343,12 +447,7 @@
         lax.fori_loop(first, first + count, body, 0)
 
     norm_rows(0, 8)
-    next_tick()
-    for copy in a2:
-        copy.wait_recv()
-    a3 = []
-    for o in range(1, 4):
-        a3.append(send(a3buf.at[q], a3buf.at[q], a3_s.at[o - 1], a3_r.at[o - 1], at_q(o)))
+    take_x(first)
     norm_rows(8, 8)
 
     de = lax.dot_general(split_ref[...], noisy_ref[...], NT, preferred_element_type=F32).astype(BF16)
@@ -356,8 +455,6 @@
         npk_ref[pl.ds(n * COLS, COLS), :] = jnp.dot(
             de[:64], place_ref[pl.ds(n * 128, 128), :], preferred_element_type=F32
         ) + jnp.dot(de[64:], place_ref[pl.ds(512 + n * 128, 128), :], preferred_element_type=F32)
-    next_tick()
-    load_taps.wait()
     for odd in range(2):
         for low in range(2):
             wb_ref[odd, :, pl.ds(512 * low, 512)] = jnp.dot(
@@ -366,11 +463,14 @@
                 preferred_element_type=F32,
             ).astype(BF16)
 
-    for copy in a3:
+    for copy in a2:
         copy.wait_recv()
-    for qq in range(4):
-        for zz in range(nz):
-            sc_ref[pl.ds(N_IMG * zz, N_IMG), pl.ds(LANES * qq, LANES)] = a3buf[qq, zz]
+    for zz in range(nz):
+        block = a2buf[zz].astype(F32)
+        for qq in range(4):
+            sc_ref[pl.ds(N_IMG * zz, N_IMG), pl.ds(LANES * qq, LANES)] = block[
+                N_IMG * qq : N_IMG * (qq + 1)
+            ]
     table = jnp.dot(sc_ref[...].astype(BF16), widen_ref[...], preferred_element_type=F32)
     half = nz // 2
     for n in range(N_IMG):
@@ -383,11 +483,12 @@
     packed = lax.dot_general(
         mod_ref[...], jnp.concatenate([proj, proj], axis=0), NT, preferred_element_type=F32
     )
-    packed = packed + projb_ref[...]
+    packed = packed + jnp.concatenate([projb_ref[...], projb_ref[...]], axis=1)
     lat_ref[...] = ((npk_ref[...] - 0.75 * packed) / 0.3611 + 0.1159).astype(BF16)
     down = send(lat_ref, halo_ref.at[0], b_s.at[0], b_r.at[0], at_s(1))
     up = send(lat_ref, halo_ref.at[1], b_s.at[1], b_r.at[1], at_s(-1))
-    next_tick()
+    take_z(second)
+    take_y_slot(own_slot, z)
 
     down.wait_recv()
     up.wait_recv()
@@ -410,8 +511,6 @@
                     )
                     + inb_ref[...]
                 ).astype(BF16)
-    next_tick()
-
     own = [(1, 0), (1, 1), (2, 0), (2, 1)]
     means, moments = [], []
     for n in range(N_IMG):
@@ -444,7 +543,7 @@
     c1 = []
     for o in range(1, 4):
         c1.append(send(c1buf.at[q], c1buf.at[q], c1_s.at[o - 1], c1_r.at[o - 1], at_q(o)))
-    next_tick()
+    take_y(first)
     for copy in c1:
         copy.wait_recv()
 
@@ -467,7 +566,7 @@
         c2.append(
             send(c2buf.at[z], c2buf.at[z], c2_s.at[o - 1], c2_r.at[o - 1], at_z(zmod(o)))
         )
-    next_tick()
+    take_x(second)
     for copy in c2:
         copy.wait_recv()
     centre, square = merge(c2buf, nz, 4.0 * 4096.0)
@@ -475,7 +574,6 @@
     both8 = jnp.where(mine, jnp.where(row8 < 4, centre, rate), 0.0)
     wide = exact_dot(both8, spread_ref[...], NN)
 
-    next_tick()
     first_row = lax.broadcasted_iota(jnp.int32, (COLS, 512), 0)
     keep_top = jnp.where(s == 0, 0.0, 1.0)
     keep_bottom = jnp.where(s == nseq - 1, 0.0, 1.0)
@@ -499,10 +597,8 @@
                 else:
                     moved = jnp.where(first_row == 0, 0.0, pltpu.roll(act, 1, 0))
                     act_ref[h, 0, at, :] = moved.astype(BF16)
-    while clock[0] <= last_tick:
-        next_tick()
-    for copy in kcopies:
-        copy.wait_recv()
+    take_y(second)
+    finish_gather()
 
     for rho in range(2):
         for part in range(2):
@@ -525,6 +621,7 @@
                     ]
     for copy in pending:
         copy.wait_send()
+    drain()
 
 
 def on_device(
@@ -550,17 +647,24 @@
     vmem = pl.BlockSpec(memory_space=pltpu.VMEM)
     hbm = pl.BlockSpec(memory_space=pl.ANY)
     dma = pltpu.SemaphoreType.DMA
-    n_plus = nz // 2
+    per = nz if ngrp == 2 else 4
+    slots = (ngrp // 2) * per + 1
     consts = [jnp.asarray(t) for t in tables()]
     scratch = [
+        pltpu.VMEM((N_IMG * ngrp, width), BF16),
+        pltpu.VMEM(mod_weight.shape[::-1], BF16),
         pltpu.VMEM((tokens, width), BF16),
-        pltpu.VMEM((1024, 144), BF16),
+        pltpu.VMEM((64, width), BF16),
+        pltpu.VMEM((128, 128), BF16),
+        pltpu.VMEM(in_weight.shape, BF16),
+        pltpu.VMEM((shard, 512), BF16),
+        *[pltpu.VMEM(t.shape, BF16) for t in consts],
         pltpu.VMEM((tokens, width), F32),
         pltpu.VMEM((tokens, width), BF16),
         pltpu.VMEM((N_IMG * nz, 512), F32),
         pltpu.VMEM((ngrp, N_IMG, LANES), F32),
-        pltpu.VMEM((ngrp, N_IMG, LANES), F32),
-        pltpu.VMEM((4, nz, N_IMG, LANES), F32),
+        pltpu.VMEM((4, ngrp, N_IMG, LANES), F32),
+        pltpu.VMEM((nz, 4 * N_IMG, LANES), BF16),
         pltpu.VMEM((tokens, LANES), F32),
         pltpu.VMEM((tokens, LANES), BF16),
         pltpu.VMEM((2, tokens, LANES), BF16),
@@ -572,33 +676,34 @@
         pltpu.VMEM((2, shard, 256), F32),
         pltpu.VMEM((shard, 256), F32),
         pltpu.VMEM((2, shard * 4 * nz, 256), BF16),
+        dma((13,)),
         dma((2,)),
-        dma((2,)),
-        dma((ngrp - 1,)),
-        dma((ngrp - 1,)),
+        dma((4 * ngrp - 1,)),
+        dma((4 * ngrp - 1,)),
         dma((nz - 1,)),
         dma((nz - 1,)),
-        dma((3,)),
-        dma((3,)),
         dma((2,)),
         dma((2,)),
         dma((3,)),
         dma((3,)),
         dma((nz - 1,)),
         dma((nz - 1,)),
-        dma((n_plus,)),
-        dma((n_plus,)),
-        dma((n_plus,)),
-        dma((n_plus,)),
-        dma((nz, 2)),
-        dma((nz, 2)),
-        dma((nz, 2)),
-        dma((nz, 2)),
+        dma((per,)),
+        dma((per,)),
+        dma((ngrp // 2, per)),
+        dma((ngrp // 2, per)),
+        dma((slots, 2)),
+        dma((slots, 2)),
+        dma((slots, 2)),
+        dma((slots, 2)),
     ]
     out = pl.pallas_call(
         functools.partial(kernel, nz, ngrp),
         out_shape=jax.ShapeDtypeStruct((N_IMG, 2, COLS, 1024), BF16),
-        in_specs=[vmem] * 3 + [hbm] + [vmem] * 9 + [hbm] + [vmem] * 5,
+        in_specs=[
+            vmem if small else hbm
+            for small in (0, 0, 1, 0, 0, 1, 0, 0, 1, 1, 1, 0, 1, 0, 0, 0, 0, 0, 0)
+        ],
         out_specs=vmem,
         scratch_shapes=scratch,
         compiler_params=pltpu.CompilerParams(
@@ -610,7 +715,7 @@
         mod_bias.reshape(1, -1),
         hidden.reshape(tokens, width),
         proj_weight.T,
-        jnp.concatenate([proj_bias, proj_bias]).reshape(1, -1),
+        proj_bias.reshape(1, -1),
         noisy_latent.transpose(0, 1, 3, 2).reshape(128, 128),
         in_weight,
         in_bias.reshape(1, -1),

time: 74 us -> 74.7 us (level)
  Pallas kernels: 70.3 us -> 72.3 us
  other arithmetic: 1.31 us -> 0 us
    pallas_call x1, Pallas kernels: 70.3 us -> 72.3 us  [on_device(): pl.pallas_call(functools.partial(kernel, nz, ngrp), out_shape=jax.ShapeDt...]
    reshape x1 -> x0, other arithmetic: 1.31 us -> none  [on_device(): jnp.concatenate([proj_bias, proj_bias]).reshape(1, -1)]
where the time goes in v2:
time: 74.7 us; the launch traced here: 74.5 us
  Pallas kernels  72.3 us (97%)
  local copies, waits for them, and re-layouts  2.2 us (3%)
    pallas_call x1, Pallas kernels, on_device(): pl.pallas_call(functools.partial(kernel, nz, ngrp), out_shape=jax.ShapeDt...  72.3 us
    reshape x1, local copies, waits for them, and re-layouts, on_device(): return out.reshape(N_IMG, 2, 2 * COLS, 512)  2.2 us

profile of v2, /device:TPU:1, one launch (start us, length us, event | category | flops | bytes accessed | tf_op | source)
XLA Modules:
  0.0 74.5 jit_solution(14665902047670779515)
XLA Ops:
  0.0 72.3 %shard_map.181 = bf16[4,2,64,1024]{3,2,1,0:T(8,128)(2,1)} custom-call(bf16[32,3072]{1,0:T(8,128)(2,1)} %cond_hbm.1, bf16[12,3072]{1,0:T(8,128)(2,1)} %bitcast.16, f32[1,12]{1,0:T(1,128)} %bitcast.22, bf16[256,3072]{1,0:T(8,128)(2,1)} %bitcast.14, bf16[64,3072]{1,0:T(8,128)(2,1)} %bitcast.15, f32[1,64]{1,0:T(1,128)} %bitcast.23, bf16[128,128]{1,0:T(8,128)(2,1)} %bitcast.17, ...), custom_call_target="tpu_custom_call" | custom-call | tf_op jit(solution)/shard_map/pallas_call | solution.py:700
  72.3 2.2 %reshape.35 = bf16[4,2,128,512]{3,2,1,0:T(8,128)(2,1)} reshape(bf16[4,2,64,1024]{3,2,1,0:T(8,128)(2,1)} %shard_map.181) | data formatting | bytes 2097152 | tf_op jit(solution)/shard_map/reshape | solution.py:728

commit v3 on v2

--- a/solution.py
+++ b/solution.py
@@ -82,17 +82,17 @@
     ngrp,
     cond_hbm,
     modw_hbm,
-    modb_ref,
+    modb_hbm,
     hid_hbm,
     projw_hbm,
-    projb_ref,
+    projb_hbm,
     noisy_hbm,
     inw_hbm,
-    inb_ref,
-    gain_ref,
-    shift_ref,
+    inb_hbm,
+    gain_hbm,
+    shift_hbm,
     convw_hbm,
-    convb_ref,
+    convb_hbm,
     taps_hbm,
     split_hbm,
     place_hbm,
@@ -113,6 +113,12 @@
     widen_ref,
     same_ref,
     spread_ref,
+    modb_ref,
+    projb_ref,
+    inb_ref,
+    gain_ref,
+    shift_ref,
+    convb_ref,
     xn_ref,
     mod_ref,
     sc_ref,
@@ -223,6 +229,7 @@
             (convw_hbm, convw_ref),
             (cond_hbm, cond_ref),
             (modw_hbm, modw_ref),
+            (modb_hbm, modb_ref),
             (hid_hbm, hid_ref),
             (noisy_hbm, noisy_ref),
             (split_hbm, split_ref),
@@ -233,12 +240,17 @@
             (widen_hbm, widen_ref),
             (same_hbm, same_ref),
             (spread_hbm, spread_ref),
+            (projb_hbm, projb_ref),
+            (inb_hbm, inb_ref),
+            (gain_hbm, gain_ref),
+            (shift_hbm, shift_ref),
+            (convb_hbm, convb_ref),
         )
     ):
         loads.append(pltpu.make_async_copy(src, dst, ld_sem.at[i]))
         loads[-1].start()
 
-    for copy in loads[:3]:
+    for copy in loads[:4]:
         copy.wait()
     rows = convw_ref.shape[0]
     whole = convw_ref[...].astype(F32)
@@ -271,7 +283,9 @@
     there = rcv_ref[...]
     top = jnp.where(core == 0, here, there)
     bottom = jnp.where(core == 0, there, here)
-    wbuf[core, chunk(z, ylo), :] = jnp.concatenate([top, bottom], axis=0).astype(BF16)
+    block = jnp.concatenate([top, bottom], axis=0).astype(BF16)
+    for p in range(2):
+        wbuf[p, core, chunk(z, ylo), :] = block[:, 128 * p : 128 * (p + 1)]
 
     nx = ngrp // 2
 
@@ -279,8 +293,8 @@
         if nx == 1:
             return j
         quarter = nz // 4
-        near = [xx, nz // 2 - xx, nz // 2 + xx, nz - xx][j]
-        return jnp.where(xx == 0, quarter * j, near)
+        steps = [xx, nz // 2 - xx, nz // 2 + xx, nz - xx][j]
+        return jnp.where(xx == 0, quarter * j, steps)
 
     def guarded(j, xx, act):
         if j == 0:
@@ -289,8 +303,7 @@
             act()
 
     per = nz if nx == 1 else 4
-    first, second = ([1], [0]) if nx == 1 else ([0, 3], [1, 2])
-
+    near, far = ([1], [0]) if nx == 1 else ([0, 3], [1, 2])
     def copy_of(src, dst, ssem, rsem, where):
         return pltpu.make_async_remote_copy(
             src_ref=src,
@@ -301,117 +314,94 @@
             device_id_type=pl.DeviceIdType.MESH,
         )
 
-    def z_copy(j):
-        at = wbuf.at[core, chunk(z, ylo)]
-        return copy_of(at, at, z_s.at[j], z_r.at[j], at_z(lax.rem(z + nz - wanted(j, x), nz)))
-
-    def x_copy(m, j):
-        at = wbuf.at[core, chunk(lax.rem(z + wanted(j, x), nz), ylo)]
-        return copy_of(at, at, x_s.at[m, j], x_r.at[m, j], at_x(m))
+    def z_copy(p, j):
+        at = wbuf.at[p, core, chunk(z, ylo)]
+        where = at_z(lax.rem(z + nz - wanted(j, x), nz))
+        return copy_of(at, at, z_s.at[p, j], z_r.at[p, j], where)
+
+    def x_copy(p, m, j):
+        at = wbuf.at[p, core, chunk(lax.rem(z + wanted(j, x), nz), ylo)]
+        return copy_of(at, at, x_s.at[p, m, j], x_r.at[p, m, j], at_x(m))
 
     def zz_of(m, j):
         return lax.rem(z + wanted(j, lax.rem(x + nx - m, nx)), nz)
 
-    def y_copies(slot, zz):
-        at = wbuf.at[core, chunk(zz, ylo)]
-        return [
-            copy_of(
-                at.at[:, pl.ds(128 * i, 128)],
-                at.at[:, pl.ds(128 * i, 128)],
-                y_s.at[slot, i],
-                y_r.at[slot, i],
-                at_y(1 - 2 * i),
-            )
-            for i in range(2)
-        ]
-
-    def k_copy(slot, zz, other):
-        at = wbuf.at[core, chunk(zz, 1 - ylo if other else ylo)]
-        return copy_of(at, at, k_s.at[slot, other], k_r.at[slot, other], mate)
-
     own_slot = nx * per
+
+    def y_copy(p, slot, zz):
+        at = wbuf.at[p, core, chunk(zz, ylo)]
+        side = 1 if (slot + p) % 2 == 0 else -1
+        return copy_of(at, at, y_s.at[p], y_r.at[p], at_y(side))
+
+    def y_total(p):
+        at = wbuf.at[p, core, pl.ds(0, 2 * rows * nz)]
+        return copy_of(at, at, y_s.at[p], y_r.at[p], at_y(1))
+
+    def k_copy(p):
+        at = wbuf.at[p, core]
+        return copy_of(at, at, k_s.at[p], k_r.at[p], mate)
+
     every = [(m, j) for m in range(nx) for j in range(per)]
 
     def origin(m):
         return lax.rem(x + nx - m, nx)
 
-    def start_own():
+    def start_z(p, js):
+        for j in js:
+            guarded(j, x, lambda j=j: z_copy(p, j).start())
+
+    def onward(p, slot, zz):
+        y_copy(p, slot, zz).start()
+
+    def start_own(p):
+        onward(p, own_slot, z)
+
+    def take_z(p, js):
+        for j in js:
+
+            def act(j=j):
+                z_copy(p, j).wait_recv()
+                for m in range(1, nx):
+                    x_copy(p, m, j).start()
+                onward(p, j, zz_of(0, j))
+
+            guarded(j, x, act)
+
+    def take_x(p, js):
+        for j in js:
+            for m in range(1, nx):
+
+                def act(m=m, j=j):
+                    x_copy(p, m, j).wait_recv()
+                    onward(p, m * per + j, zz_of(m, j))
+
+                guarded(j, origin(m), act)
+
+    def take_y(p):
+        y_total(p).wait_recv()
+        k_copy(p).start()
+
+    def finish_gather(p):
+        k_copy(p).wait_recv()
+
+    def drain(p):
         for j in range(per):
-            guarded(j, x, lambda j=j: z_copy(j).start())
-        for copy in y_copies(own_slot, z):
-            copy.start()
-        k_copy(own_slot, z, 0).start()
-
-    def onward(m, j):
-        for copy in y_copies(m * per + j, zz_of(m, j)):
-            copy.start()
-        k_copy(m * per + j, zz_of(m, j), 0).start()
-
-    def take_z(js):
-        for j in js:
-
-            def act(j=j):
-                z_copy(j).wait_recv()
+
+            def sent(j=j):
+                z_copy(p, j).wait_send()
                 for m in range(1, nx):
-                    x_copy(m, j).start()
-                onward(0, j)
-
-            guarded(j, x, act)
-
-    def take_x(js):
-        for m in range(1, nx):
-            for j in js:
-
-                def act(m=m, j=j):
-                    x_copy(m, j).wait_recv()
-                    onward(m, j)
-
-                guarded(j, origin(m), act)
-
-    def take_y_slot(slot, zz):
-        for copy in y_copies(slot, zz):
-            copy.wait_recv()
-        k_copy(slot, zz, 1).start()
-
-    def take_y(js):
-        for m in range(nx):
-            for j in js:
-                guarded(j, origin(m), lambda m=m, j=j: take_y_slot(m * per + j, zz_of(m, j)))
-
-    def finish_gather():
-        for other in range(2):
-            k_copy(own_slot, z, other).wait_recv()
-            for m, j in every:
-                guarded(
-                    j,
-                    origin(m),
-                    lambda m=m, j=j: k_copy(m * per + j, zz_of(m, j), other).wait_recv(),
-                )
-
-    def drain():
-        for j in range(per):
-
-            def sent(j=j):
-                z_copy(j).wait_send()
-                for m in range(1, nx):
-                    x_copy(m, j).wait_send()
+                    x_copy(p, m, j).wait_send()
 
             guarded(j, x, sent)
-        for copy in y_copies(own_slot, z):
-            copy.wait_send()
-        for other in range(2):
-            k_copy(own_slot, z, other).wait_send()
-        for m, j in every:
-
-            def sent(m=m, j=j):
-                for copy in y_copies(m * per + j, zz_of(m, j)):
-                    copy.wait_send()
-                for other in range(2):
-                    k_copy(m * per + j, zz_of(m, j), other).wait_send()
-
-            guarded(j, origin(m), sent)
-
-    start_own()
+        y_total(p).wait_send()
+        k_copy(p).wait_send()
+
+    def flush():
+        while pending:
+            pending.pop().wait_send()
+
+    start_z(0, far + near)
+    start_z(1, near)
 
     for copy in a1:
         copy.wait_recv()
@@ -431,8 +421,8 @@
             send(a2buf.at[z], a2buf.at[z], a2_s.at[o - 1], a2_r.at[o - 1], at_z(zmod(o)))
         )
 
-    take_z(first)
-    for copy in loads[3:]:
+    start_own(0)
+    for copy in loads[4:]:
         copy.wait()
 
     def norm_rows(first, count):
@@ -447,8 +437,9 @@
         lax.fori_loop(first, first + count, body, 0)
 
     norm_rows(0, 8)
-    take_x(first)
+    take_z(0, near + far)
     norm_rows(8, 8)
+    take_z(1, near)
 
     de = lax.dot_general(split_ref[...], noisy_ref[...], NT, preferred_element_type=F32).astype(BF16)
     for n in range(N_IMG):
@@ -487,11 +478,10 @@
     lat_ref[...] = ((npk_ref[...] - 0.75 * packed) / 0.3611 + 0.1159).astype(BF16)
     down = send(lat_ref, halo_ref.at[0], b_s.at[0], b_r.at[0], at_s(1))
     up = send(lat_ref, halo_ref.at[1], b_s.at[1], b_r.at[1], at_s(-1))
-    take_z(second)
-    take_y_slot(own_slot, z)
-
+    flush()
     down.wait_recv()
     up.wait_recv()
+    start_z(1, far)
     lat = lat_ref[...].astype(F32)
     above = jnp.where(s == 0, 0.0, halo_ref[0].astype(F32))
     below = jnp.where(s == nseq - 1, 0.0, halo_ref[1].astype(F32))
@@ -543,7 +533,6 @@
     c1 = []
     for o in range(1, 4):
         c1.append(send(c1buf.at[q], c1buf.at[q], c1_s.at[o - 1], c1_r.at[o - 1], at_q(o)))
-    take_y(first)
     for copy in c1:
         copy.wait_recv()
 
@@ -566,7 +555,12 @@
         c2.append(
             send(c2buf.at[z], c2buf.at[z], c2_s.at[o - 1], c2_r.at[o - 1], at_z(zmod(o)))
         )
-    take_x(second)
+    take_x(0, near + far)
+    start_own(1)
+    take_x(1, near)
+    take_z(1, far)
+    take_y(0)
+    take_x(1, far)
     for copy in c2:
         copy.wait_recv()
     centre, square = merge(c2buf, nz, 4.0 * 4096.0)
@@ -597,31 +591,37 @@
                 else:
                     moved = jnp.where(first_row == 0, 0.0, pltpu.roll(act, 1, 0))
                     act_ref[h, 0, at, :] = moved.astype(BF16)
-    take_y(second)
-    finish_gather()
-
-    for rho in range(2):
-        for part in range(2):
+    flush()
+    finish_gather(0)
+    drain(0)
+
+    for p in range(2):
+        bias = jnp.concatenate(
+            [convb_ref[:, pl.ds(128 * p, 128)], convb_ref[:, pl.ds(256 + 128 * p, 128)]], axis=1
+        )
+        for rho in range(2):
             acc = None
             for a in range(3):
                 for b in range(3):
                     lhs = act_ref[rho + a, pl.ds(b, 2)].reshape(2 * N_IMG * COLS, 512)
-                    term = jnp.dot(
-                        lhs,
-                        wbuf[part, pl.ds((3 * a + b) * 512, 512), :],
-                        preferred_element_type=F32,
-                    )
+                    depth = pl.ds((3 * a + b) * 512, 512)
+                    rhs = jnp.concatenate([wbuf[p, 0, depth, :], wbuf[p, 1, depth, :]], axis=1)
+                    term = jnp.dot(lhs, rhs, preferred_element_type=F32)
                     acc = term if acc is None else acc + term
-            acc = (acc + convb_ref[:, pl.ds(256 * part, 256)]).astype(BF16)
+            acc = (acc + bias).astype(BF16)
             for odd in range(2):
                 for n in range(N_IMG):
-                    first = (odd * N_IMG + n) * COLS
-                    out_ref[n, rho, :, pl.ds(512 * odd + 256 * part, 256)] = acc[
-                        first : first + COLS
-                    ]
-    for copy in pending:
-        copy.wait_send()
-    drain()
+                    row = (odd * N_IMG + n) * COLS
+                    for part in range(2):
+                        at = pl.ds(512 * odd + 256 * part + 128 * p, 128)
+                        out_ref[n, rho, :, at] = acc[
+                            row : row + COLS, 128 * part : 128 * (part + 1)
+                        ]
+            if p == 0 and rho == 0:
+                take_y(1)
+            if p == 0 and rho == 1:
+                finish_gather(1)
+    drain(1)
 
 
 def on_device(
@@ -648,7 +648,6 @@
     hbm = pl.BlockSpec(memory_space=pl.ANY)
     dma = pltpu.SemaphoreType.DMA
     per = nz if ngrp == 2 else 4
-    slots = (ngrp // 2) * per + 1
     consts = [jnp.asarray(t) for t in tables()]
     scratch = [
         pltpu.VMEM((N_IMG * ngrp, width), BF16),
@@ -659,6 +658,7 @@
         pltpu.VMEM(in_weight.shape, BF16),
         pltpu.VMEM((shard, 512), BF16),
         *[pltpu.VMEM(t.shape, BF16) for t in consts],
+        *[pltpu.VMEM((1, n), F32) for n in (mod_weight.shape[1], 64, 512, 512, 512, 512)],
         pltpu.VMEM((tokens, width), F32),
         pltpu.VMEM((tokens, width), BF16),
         pltpu.VMEM((N_IMG * nz, 512), F32),
@@ -675,8 +675,8 @@
         pltpu.VMEM((nz, 2, LANES), F32),
         pltpu.VMEM((2, shard, 256), F32),
         pltpu.VMEM((shard, 256), F32),
-        pltpu.VMEM((2, shard * 4 * nz, 256), BF16),
-        dma((13,)),
+        pltpu.VMEM((2, 2, shard * 4 * nz, 128), BF16),
+        dma((19,)),
         dma((2,)),
         dma((4 * ngrp - 1,)),
         dma((4 * ngrp - 1,)),
@@ -688,22 +688,19 @@
         dma((3,)),
         dma((nz - 1,)),
         dma((nz - 1,)),
-        dma((per,)),
-        dma((per,)),
-        dma((ngrp // 2, per)),
-        dma((ngrp // 2, per)),
-        dma((slots, 2)),
-        dma((slots, 2)),
-        dma((slots, 2)),
-        dma((slots, 2)),
+        dma((2, per)),
+        dma((2, per)),
+        dma((2, ngrp // 2, per)),
+        dma((2, ngrp // 2, per)),
+        dma((2,)),
+        dma((2,)),
+        dma((2,)),
+        dma((2,)),
     ]
     out = pl.pallas_call(
         functools.partial(kernel, nz, ngrp),
         out_shape=jax.ShapeDtypeStruct((N_IMG, 2, COLS, 1024), BF16),
-        in_specs=[
-            vmem if small else hbm
-            for small in (0, 0, 1, 0, 0, 1, 0, 0, 1, 1, 1, 0, 1, 0, 0, 0, 0, 0, 0)
-        ],
+        in_specs=[hbm] * 19,
         out_specs=vmem,
         scratch_shapes=scratch,
         compiler_params=pltpu.CompilerParams(

time: 74.7 us -> 66.3 us (0.89)
  Pallas kernels: 72.3 us -> 63.8 us
    pallas_call x1, Pallas kernels: 72.3 us -> 63.8 us  [on_device(): pl.pallas_call(functools.partial(kernel, nz, ngrp), out_shape=jax.ShapeDt...]
where the time goes in v3:
time: 66.3 us; the launch traced here: 66 us
  Pallas kernels  63.8 us (96%)
  local copies, waits for them, and re-layouts  2.2 us (3%)
    pallas_call x1, Pallas kernels, on_device(): pl.pallas_call(functools.partial(kernel, nz, ngrp), out_shape=jax.ShapeDt...  63.8 us
    reshape x1, local copies, waits for them, and re-layouts, on_device(): return out.reshape(N_IMG, 2, 2 * COLS, 512)  2.2 us

profile of v3, /device:TPU:1, one launch (start us, length us, event | category | flops | bytes accessed | tf_op | source)
XLA Modules:
  0.0 66.0 jit_solution(5180026208782836496)
XLA Ops:
  0.0 63.8 %shard_map.181 = bf16[4,2,64,1024]{3,2,1,0:T(8,128)(2,1)} custom-call(bf16[32,3072]{1,0:T(8,128)(2,1)} %cond_hbm.1, bf16[12,3072]{1,0:T(8,128)(2,1)} %bitcast.16, f32[1,12]{1,0:T(1,128)} %bitcast.22, bf16[256,3072]{1,0:T(8,128)(2,1)} %bitcast.14, bf16[64,3072]{1,0:T(8,128)(2,1)} %bitcast.15, f32[1,64]{1,0:T(1,128)} %bitcast.23, bf16[128,128]{1,0:T(8,128)(2,1)} %bitcast.17, ...), custom_call_target="tpu_custom_call" | custom-call | tf_op jit(solution)/shard_map/pallas_call | solution.py:700
  63.8 2.2 %reshape.35 = bf16[4,2,128,512]{3,2,1,0:T(8,128)(2,1)} reshape(bf16[4,2,64,1024]{3,2,1,0:T(8,128)(2,1)} %shard_map.181) | data formatting | bytes 2097152 | tf_op jit(solution)/shard_map/reshape | solution.py:725

commit v4 on v3

--- a/solution.py
+++ b/solution.py
@@ -400,8 +400,30 @@
         while pending:
             pending.pop().wait_send()
 
-    start_z(0, far + near)
-    start_z(1, near)
+    start_z(0, near)
+    start_z(0, far)
+
+    for copy in loads[4:]:
+        copy.wait()
+
+    def norm_rows(first, count):
+        def body(step, carry):
+            at = pl.ds(pl.multiple_of(step * 16, 16), 16)
+            h = hid_ref[at, :].astype(F32)
+            c = h - jnp.mean(h, axis=-1, keepdims=True)
+            var = jnp.mean(c * c, axis=-1, keepdims=True)
+            xn_ref[at, :] = c * lax.rsqrt(var + 1e-06)
+            return carry
+
+        lax.fori_loop(first, first + count, body, 0)
+
+    norm_rows(0, 16)
+
+    de = lax.dot_general(split_ref[...], noisy_ref[...], NT, preferred_element_type=F32).astype(BF16)
+    for n in range(N_IMG):
+        npk_ref[pl.ds(n * COLS, COLS), :] = jnp.dot(
+            de[:64], place_ref[pl.ds(n * 128, 128), :], preferred_element_type=F32
+        ) + jnp.dot(de[64:], place_ref[pl.ds(512 + n * 128, 128), :], preferred_element_type=F32)
 
     for copy in a1:
         copy.wait_recv()
@@ -422,30 +444,7 @@
         )
 
     start_own(0)
-    for copy in loads[4:]:
-        copy.wait()
-
-    def norm_rows(first, count):
-        def body(step, carry):
-            at = pl.ds(pl.multiple_of(step * 16, 16), 16)
-            h = hid_ref[at, :].astype(F32)
-            c = h - jnp.mean(h, axis=-1, keepdims=True)
-            var = jnp.mean(c * c, axis=-1, keepdims=True)
-            xn_ref[at, :] = c * lax.rsqrt(var + 1e-06)
-            return carry
-
-        lax.fori_loop(first, first + count, body, 0)
-
-    norm_rows(0, 8)
-    take_z(0, near + far)
-    norm_rows(8, 8)
-    take_z(1, near)
-
-    de = lax.dot_general(split_ref[...], noisy_ref[...], NT, preferred_element_type=F32).astype(BF16)
-    for n in range(N_IMG):
-        npk_ref[pl.ds(n * COLS, COLS), :] = jnp.dot(
-            de[:64], place_ref[pl.ds(n * 128, 128), :], preferred_element_type=F32
-        ) + jnp.dot(de[64:], place_ref[pl.ds(512 + n * 128, 128), :], preferred_element_type=F32)
+    take_z(0, near)
     for odd in range(2):
         for low in range(2):
             wb_ref[odd, :, pl.ds(512 * low, 512)] = jnp.dot(
@@ -454,6 +453,8 @@
                 preferred_element_type=F32,
             ).astype(BF16)
 
+    take_x(0, near)
+    take_z(0, far)
     for copy in a2:
         copy.wait_recv()
     for zz in range(nz):
@@ -478,29 +479,41 @@
     lat_ref[...] = ((npk_ref[...] - 0.75 * packed) / 0.3611 + 0.1159).astype(BF16)
     down = send(lat_ref, halo_ref.at[0], b_s.at[0], b_r.at[0], at_s(1))
     up = send(lat_ref, halo_ref.at[1], b_s.at[1], b_r.at[1], at_s(-1))
+    start_z(1, near)
+    start_z(1, far)
     flush()
     down.wait_recv()
     up.wait_recv()
-    start_z(1, far)
+    take_x(0, far)
+    start_own(1)
     lat = lat_ref[...].astype(F32)
     above = jnp.where(s == 0, 0.0, halo_ref[0].astype(F32))
     below = jnp.where(s == nseq - 1, 0.0, halo_ref[1].astype(F32))
     left = lax.broadcasted_iota(jnp.int32, (N_IMG * COLS, LANES), 1) < 64
     column = lax.rem(lax.broadcasted_iota(jnp.int32, (N_IMG * COLS, LANES), 0), COLS)
+    patches = {}
     for pair in range(2):
         both = jnp.where(left, above, lat) if pair == 0 else jnp.where(left, lat, below)
         before = jnp.where(column == 0, 0.0, pltpu.roll(both, 1, 0))
         after = jnp.where(column == COLS - 1, 0.0, pltpu.roll(both, N_IMG * COLS - 1, 0))
         for odd in range(2):
             parts = [before, both] if odd == 0 else [both, after]
-            patch = jnp.concatenate(parts, axis=1).astype(BF16)
-            for low in range(2):
-                feat_ref[2 * pair + low, odd] = (
-                    jnp.dot(
-                        patch, wb_ref[odd, :, pl.ds(512 * low, 512)], preferred_element_type=F32
-                    )
-                    + inb_ref[...]
-                ).astype(BF16)
+            patches[pair, odd] = jnp.concatenate(parts, axis=1).astype(BF16)
+
+    def make_features(pair, low):
+        for odd in range(2):
+            feat_ref[2 * pair + low, odd] = (
+                jnp.dot(
+                    patches[pair, odd],
+                    wb_ref[odd, :, pl.ds(512 * low, 512)],
+                    preferred_element_type=F32,
+                )
+                + inb_ref[...]
+            ).astype(BF16)
+
+    make_features(0, 1)
+    make_features(1, 0)
+
     own = [(1, 0), (1, 1), (2, 0), (2, 1)]
     means, moments = [], []
     for n in range(N_IMG):
@@ -533,6 +546,9 @@
     c1 = []
     for o in range(1, 4):
         c1.append(send(c1buf.at[q], c1buf.at[q], c1_s.at[o - 1], c1_r.at[o - 1], at_q(o)))
+    take_z(1, near)
+    make_features(0, 0)
+    make_features(1, 1)
     for copy in c1:
         copy.wait_recv()
 
@@ -555,12 +571,10 @@
         c2.append(
             send(c2buf.at[z], c2buf.at[z], c2_s.at[o - 1], c2_r.at[o - 1], at_z(zmod(o)))
         )
-    take_x(0, near + far)
-    start_own(1)
+    take_z(1, far)
     take_x(1, near)
-    take_z(1, far)
+    take_x(1, far)
     take_y(0)
-    take_x(1, far)
     for copy in c2:
         copy.wait_recv()
     centre, square = merge(c2buf, nz, 4.0 * 4096.0)

time: 66.3 us -> 64.4 us (0.971)
  Pallas kernels: 63.8 us -> 62.1 us
    pallas_call x1, Pallas kernels: 63.8 us -> 62.1 us  [on_device(): pl.pallas_call(functools.partial(kernel, nz, ngrp), out_shape=jax.ShapeDt...]
where the time goes in v4:
time: 64.4 us; the launch traced here: 64.3 us
  Pallas kernels  62.1 us (96%)
  local copies, waits for them, and re-layouts  2.2 us (3%)
    pallas_call x1, Pallas kernels, on_device(): pl.pallas_call(functools.partial(kernel, nz, ngrp), out_shape=jax.ShapeDt...  62.1 us
    reshape x1, local copies, waits for them, and re-layouts, on_device(): return out.reshape(N_IMG, 2, 2 * COLS, 512)  2.2 us

profile of v4, /device:TPU:1, one launch (start us, length us, event | category | flops | bytes accessed | tf_op | source)
XLA Modules:
  0.0 64.3 jit_solution(12477628429398039052)
XLA Ops:
  0.0 62.1 %shard_map.181 = bf16[4,2,64,1024]{3,2,1,0:T(8,128)(2,1)} custom-call(bf16[32,3072]{1,0:T(8,128)(2,1)} %cond_hbm.1, bf16[12,3072]{1,0:T(8,128)(2,1)} %bitcast.16, f32[1,12]{1,0:T(1,128)} %bitcast.22, bf16[256,3072]{1,0:T(8,128)(2,1)} %bitcast.14, bf16[64,3072]{1,0:T(8,128)(2,1)} %bitcast.15, f32[1,64]{1,0:T(1,128)} %bitcast.23, bf16[128,128]{1,0:T(8,128)(2,1)} %bitcast.17, ...), custom_call_target="tpu_custom_call" | custom-call | tf_op jit(solution)/shard_map/pallas_call | solution.py:714
  62.1 2.2 %reshape.35 = bf16[4,2,128,512]{3,2,1,0:T(8,128)(2,1)} reshape(bf16[4,2,64,1024]{3,2,1,0:T(8,128)(2,1)} %shard_map.181) | data formatting | bytes 2097152 | tf_op jit(solution)/shard_map/reshape | solution.py:739
